TPU v7x, 32 devices: a whole 2x2x4 slice. The times are simulated.
32 devices in a mesh: groups: 2 (over y), row: 4 (over z), col: 4 (over x, core).
Axes of the slice: x: 2, y: 2, z: 4, core: 2. Of those that a mesh axis runs over, the one named last changes fastest.
Arguments:
- right_side: float32 [4096, 512], P(('groups', 'row')), parts along dimension 0, may hold values from -6 to 6
- prev_factor: float32 [4096, 4096], P(('groups', 'row'), 'col'), parts along dimension 0, may hold values from -0.09375 to 0.09375
- prev_solution: float32 [8192, 512], P(('groups', 'col'), 'row'), parts along dimension 0, may hold values from -6 to 6
- window_factor: float32 [4096, 1536], P(('groups', 'row')), parts along dimension 0, may hold values from -2 to 2
Outputs:
- panel: float32 [4096, 512], P(('groups', 'row'), 'col'), parts along dimension 0
There are 2 independent parts, one for each index of `groups`. A program takes and returns all parts, laid end to end along the dimension named above; each array names one. Nothing has to cross between parts.
All inputs are finite; a program needn't handle non-finite values.
Results may differ from a plain program's by a relative error of at most 0.0001.
Values sent between devices are 32-bit elements; how exact they have to be, the bound alone decides.
A program may use at most 64 MiB of HBM per device.

v0:
```python
import jax
import jax.numpy as jnp
from jax import lax
from jax.sharding import PartitionSpec as P

NRHS = 512
STEPS = 6


def spread(array, axis, root):
    mine = lax.axis_index(axis) == root
    return lax.psum(jnp.where(mine, array, jnp.zeros_like(array)), axis)


def advance(resid, tiles, order, step, slot, is_root, sender):
    local = resid[slot]

    def solve_tile():
        return jnp.dot(
            tiles[slot, :, step, :],
            local,
            precision=lax.Precision.HIGHEST,
            preferred_element_type=jnp.float32,
        )

    def empty_tile():
        return jnp.zeros_like(local)

    mine = lax.cond(is_root, solve_tile, empty_tile)
    solved = sender(mine)
    update = jnp.einsum(
        "sij,jn->sin", tiles[:, :, step, :], solved, precision=lax.Precision.HIGHEST
    )
    later = (order > step)[:, None, None]
    resid = jnp.where(later, resid - update, resid)
    resid = jnp.where((order == step)[:, None, None], solved[None], resid)
    return resid


def body(right_side, prev_factor, prev_solution, window_factor):
    row_count = lax.axis_size("row")
    row_index = lax.axis_index("row")
    col_count = lax.axis_size("col")
    col_index = lax.axis_index("col")
    blocks = window_factor.shape[1] // STEPS
    slots = right_side.shape[0] // blocks
    partial_value = jnp.dot(
        prev_factor,
        lax.all_gather(prev_solution, "row", axis=1, tiled=True),
        precision=lax.Precision.HIGHEST,
        preferred_element_type=jnp.float32,
    )
    tiles = window_factor.reshape(slots, blocks, STEPS, blocks)
    order = jnp.arange(slots, dtype=jnp.int32) * row_count + row_index
    prior = lax.psum(partial_value, "col")
    resid = (right_side - prior).reshape(slots, blocks, -1)
    for step in range(STEPS):
        root = step % row_count
        resid = advance(
            resid,
            tiles,
            order,
            step,
            step // row_count,
            row_index == root,
            lambda solved: spread(solved, "row", root),
        )
    width = NRHS // col_count
    return lax.dynamic_slice_in_dim(resid.reshape(slots * blocks, -1), col_index * width, width, 1)


def solution(mesh):
    in_specs = (
        P(("groups", "row"), None),
        P(("groups", "row"), "col"),
        P(("groups", "col"), "row"),
        P(("groups", "row"), None),
    )
    out_specs = P(("groups", "row"), "col")
    return jax.shard_map(body, mesh=mesh, in_specs=in_specs, out_specs=out_specs, check_vma=False)
```

profile of v0, /device:TPU:27, one launch (start us, length us, event | category | flops | bytes accessed | tf_op | source)
XLA Modules:
  0.0 410.7 jit_solution(410126882840946337)
XLA Ops:
  7.3 46.3 %all-gather.2.cloned.1.call-done = f32[1024,512]{1,0:T(8,128)} async-done(((f32[1024,128]{1,0:T(8,128)}), f32[1024,512]{1,0:T(8,128)}) %all-gather.2.cloned.1.call-update) | async-done | bytes 2097168 | tf_op jit(solution)/shard_map/all_gather | solution.py:49
  53.6 6.1 %fusion.48 = f32[512,512]{1,0:T(8,128)} fusion(f32[512,1024]{1,0:T(8,128)S(1)} %copy-done, f32[1024,512]{1,0:T(8,128)} %all-gather.2.cloned.1.call-done), kind=kOutput, calls=%fused_computation.80 | convolution fusion | flops 3221225472 | bytes 5242880 | tf_op jit(solution)/shard_map/dot_general | solution.py:47
  59.8 3.5 copy.11
  63.3 3.8 reshape.56
  67.1 29.1 %all-reduce.8.cloned.1.call-done = f32[512,512]{1,0:T(8,128)} async-done(((f32[512,512]{1,0:T(8,128)}), f32[512,512]{1,0:T(8,128)}) %all-reduce.8.cloned.1.call-update) | async-done | bytes 1048592 | tf_op jit(solution)/shard_map/psum | solution.py:55
  96.1 2.8 sub.21
  98.9 0.9 conditional.6
  100.6 2.4 fusion.47
  103.0 2.0 copy.30
  105.1 38.3 %all-reduce.10.cloned.1.call-done = f32[256,512]{1,0:T(8,128)} async-done(((f32[256,512]{1,0:T(8,128)}), f32[256,512]{1,0:T(8,128)}) %all-reduce.10.cloned.1.call-update) | async-done | bytes 524304 | tf_op jit(solution)/shard_map/psum | solution.py:12
  143.4 3.8 fusion.34
  148.9 2.0 copy.31
  151.0 43.6 %all-reduce.12.cloned.1.call-done = f32[256,512]{1,0:T(8,128)} async-done(((f32[256,512]{1,0:T(8,128)}), f32[256,512]{1,0:T(8,128)}) %all-reduce.12.cloned.1.call-update) | async-done | bytes 524304 | tf_op jit(solution)/shard_map/psum | solution.py:12
  194.6 3.7 fusion.33
  198.3 0.9 conditional.8
  200.1 2.0 copy.32
  202.2 44.4 %all-reduce.14.cloned.1.call-done = f32[256,512]{1,0:T(8,128)} async-done(((f32[256,512]{1,0:T(8,128)}), f32[256,512]{1,0:T(8,128)}) %all-reduce.14.cloned.1.call-update) | async-done | bytes 524304 | tf_op jit(solution)/shard_map/psum | solution.py:12
  246.5 3.7 fusion.32
  250.3 8.2 %conditional.9 = (f32[256,512]{1,0:T(8,128)}) conditional(s32[]{:T(128)} %convert_element_type.16, () %tuple.43, (f32[2,256,6,256]{1,0,3,2:T(2,128)S(1)}, f32[2,256,512]{2,1,0:T(8,128)}) %tuple.50), branch_computations={%region_10.11_spmd, %region_11.12_spmd} | conditional | flops 402653184 | bytes 8126472 | solution.py:29
  250.3 3.9 copy.18
  254.2 1.9 slice.70
  256.0 2.5 fusion.14
  258.5 1.9 broadcast_select_fusion.2
  260.5 2.0 copy.33
  262.5 36.3 %all-reduce.16.cloned.1.call-done = f32[256,512]{1,0:T(8,128)} async-done(((f32[256,512]{1,0:T(8,128)}), f32[256,512]{1,0:T(8,128)}) %all-reduce.16.cloned.1.call-update) | async-done | bytes 524304 | tf_op jit(solution)/shard_map/psum | solution.py:12
  298.8 3.7 fusion.31
  304.4 2.0 copy.34
  306.4 42.9 %all-reduce.18.cloned.1.call-done = f32[256,512]{1,0:T(8,128)} async-done(((f32[256,512]{1,0:T(8,128)}), f32[256,512]{1,0:T(8,128)}) %all-reduce.18.cloned.1.call-update) | async-done | bytes 524304 | tf_op jit(solution)/shard_map/psum | solution.py:12
  349.3 3.7 fusion.30
  354.8 2.3 copy.35
  357.1 43.5 %all-reduce.20.cloned.1.call-done = f32[256,512]{1,0:T(8,128)} async-done(((f32[256,512]{1,0:T(8,128)}), f32[256,512]{1,0:T(8,128)}) %all-reduce.20.cloned.1.call-update) | async-done | bytes 524304 | tf_op jit(solution)/shard_map/psum | solution.py:12
  400.7 2.5 fusion.29
  (42 shorter events, 13.0 us)
Async XLA Ops:
  6.5 47.0 %copy-start = (f32[512,1024]{1,0:T(8,128)S(1)}, f32[512,1024]{1,0:T(8,128)}, u32[]{:S(2)}) copy-start(f32[512,1024]{1,0:T(8,128)} %param.17) | copy-start | bytes 6291460
  6.5 47.0 %all-gather.2.cloned.1.call-start = ((), (), s32[]{:S(2)}) async-start(), calls=%async_computation | async-start | bytes 2621440 | tf_op jit(solution)/shard_map/all_gather | solution.py:49
  7.3 88.9 %all-reduce.8.cloned.1.call-start = ((), (), s32[]{:S(2)}) async-start(), calls=%async_computation.1 | async-start | bytes 2097152 | tf_op jit(solution)/shard_map/psum | solution.py:55
  59.7 83.7 %all-reduce.10.cloned.1.call-start = ((), (), s32[]{:S(2)}) async-start(), calls=%async_computation.2 | async-start | bytes 1048576 | tf_op jit(solution)/shard_map/psum | solution.py:12
  100.6 94.0 %all-reduce.12.cloned.1.call-start = ((), (), s32[]{:S(2)}) async-start(), calls=%async_computation.3 | async-start | bytes 1048576 | tf_op jit(solution)/shard_map/psum | solution.py:12
  148.9 97.6 %all-reduce.14.cloned.1.call-start = ((), (), s32[]{:S(2)}) async-start(), calls=%async_computation.4 | async-start | bytes 1048576 | tf_op jit(solution)/shard_map/psum | solution.py:12
  200.1 98.8 %all-reduce.16.cloned.1.call-start = ((), (), s32[]{:S(2)}) async-start(), calls=%async_computation.5 | async-start | bytes 1048576 | tf_op jit(solution)/shard_map/psum | solution.py:12
  260.4 88.9 %all-reduce.18.cloned.1.call-start = ((), (), s32[]{:S(2)}) async-start(), calls=%async_computation.6 | async-start | bytes 1048576 | tf_op jit(solution)/shard_map/psum | solution.py:12
  304.3 96.3 %all-reduce.20.cloned.1.call-start = ((), (), s32[]{:S(2)}) async-start(), calls=%async_computation.7 | async-start | bytes 1048576 | tf_op jit(solution)/shard_map/psum | solution.py:12
  353.9 46.7 %copy-start.2 = (f32[2,256,512]{2,1,0:T(8,128)S(1)}, f32[2,256,512]{2,1,0:T(8,128)}, u32[]{:S(2)}) copy-start(f32[2,256,512]{2,1,0:T(8,128)} %fusion.30) | copy-start | bytes 3145732
  353.9 49.9 %copy-start.1 = (f32[512,1024]{1,0:T(8,128)S(1)}, f32[512,1024]{1,0:T(8,128)}, u32[]{:S(2)}) copy-start(f32[512,1024]{1,0:T(8,128)} %param.17) | copy-start | bytes 6291460
Sparse Core Ops, SparseCore 0:
  8.9 44.6 all-gather.1
  59.8 36.2 all-reduce.7
  100.7 42.6 all-reduce.9
  149.0 45.5 all-reduce.11
  200.2 46.2 all-reduce.13
  260.5 38.2 all-reduce.15
  304.4 44.8 all-reduce.17
  354.9 45.6 all-reduce.19
where the time goes:
time: 416 us; the launch traced here: 411 us
  waiting for transfers between devices  325 us (78%)
  local copies, waits for them, and re-layouts  33.1 us (8%)
  matrix products  29.8 us (7%)
  between operations  13.5 us (3%)
  other arithmetic  8.89 us (2%)
    psum x6, waiting for transfers between devices, spread(): return lax.psum(jnp.where(mine, array, jnp.zeros_like(array)), axis)  249 us
    all_gather x1, waiting for transfers between devices, body(): lax.all_gather(prev_solution, 'row', axis=1, tiled=True)  46.3 us
    psum x1, waiting for transfers between devices, body(): prior = lax.psum(partial_value, 'col')  29.1 us
    dot_general x6, matrix products, advance(): jnp.einsum('sij,jn->sin', tiles[:, :, step, :], solved, precision=lax.Pre...  21.2 us
    unnamed x13, local copies, waits for them, and re-layouts  16.1 us
  transfers between devices with their start and end apart: 8, of which 8 were waited for; matrix products, arithmetic and copies ran while one was open for 5% of the time, Pallas kernels for 0%

commit v1 on v0

v1 whole, which is shorter than its diff:
```python
import functools

import jax
import jax.numpy as jnp
from jax import lax
from jax.experimental import pallas as pl
from jax.experimental.pallas import tpu as pltpu
from jax.sharding import PartitionSpec as P

STEPS = 6
MESH = pl.DeviceIdType.MESH


def general_body(right_side, prev_factor, prev_solution, window_factor):
    row_count = lax.axis_size("row")
    row_index = lax.axis_index("row")
    col_count = lax.axis_size("col")
    col_index = lax.axis_index("col")
    blocks = window_factor.shape[1] // STEPS
    slots = right_side.shape[0] // blocks
    width = right_side.shape[1] // col_count
    partial_value = jnp.dot(
        prev_factor,
        lax.all_gather(prev_solution, "row", axis=1, tiled=True),
        precision=lax.Precision.HIGHEST,
        preferred_element_type=jnp.float32,
    )
    prior = lax.psum_scatter(partial_value, "col", scatter_dimension=1, tiled=True)
    mine = lax.dynamic_slice_in_dim(right_side, col_index * width, width, 1)
    resid = (mine - prior).reshape(slots, blocks, width)
    tiles = window_factor.reshape(slots, blocks, STEPS, blocks)
    order = jnp.arange(slots, dtype=jnp.int32) * row_count + row_index
    for step in range(STEPS):
        root, slot = step % row_count, step // row_count
        solved = jnp.dot(
            tiles[slot, :, step, :],
            resid[slot],
            precision=lax.Precision.HIGHEST,
            preferred_element_type=jnp.float32,
        )
        solved = lax.psum(jnp.where(row_index == root, solved, 0.0), "row")
        update = jnp.einsum(
            "sij,jn->sin", tiles[:, :, step, :], solved, precision=lax.Precision.HIGHEST
        )
        resid = jnp.where((order > step)[:, None, None], resid - update, resid)
        resid = jnp.where((order == step)[:, None, None], solved[None], resid)
    return resid.reshape(slots * blocks, width)


def halves(value):
    high = value.astype(jnp.bfloat16)
    low = (value - high.astype(jnp.float32)).astype(jnp.bfloat16)
    return high, low


def dot3(a_high, a_low, b):
    b_high, b_low = halves(b)
    dot = functools.partial(jnp.dot, preferred_element_type=jnp.float32)
    return dot(a_high, b_high) + (dot(a_high, b_low) + dot(a_low, b_high))


def kernel(
    rows, cols, slots, bk, chunks, width,
    right_ref, factor_ref, solution_ref, window_ref, out_ref,
    factor, factor_high, factor_low, window, window_high, window_low,
    xs, parts, arrived, resid, solved,
    load_sem, gather_send, gather_recv, part_send, part_recv, solved_send, solved_recv,
):
    z = lax.axis_index("row")
    c = lax.axis_index("col")
    depth = xs.shape[2]
    last_slot = slots - 1

    barrier = pltpu.get_barrier_semaphore()
    for i in range(1, rows):
        pl.semaphore_signal(barrier, inc=1, device_id={"row": lax.rem(z + i, rows)}, device_id_type=MESH)
    for i in range(1, cols):
        pl.semaphore_signal(barrier, inc=1, device_id={"col": lax.rem(c + i, cols)}, device_id_type=MESH)

    load_x = [
        pltpu.make_async_copy(solution_ref.at[pl.ds(q * depth, depth)], xs.at[z, q], load_sem.at[q])
        for q in range(chunks)
    ]
    load_factor = [
        pltpu.make_async_copy(
            factor_ref.at[:, pl.ds(q * depth, depth)], factor.at[q], load_sem.at[chunks + q]
        )
        for q in range(chunks)
    ]
    column = pl.multiple_of(c * width, width)
    load_right = [
        pltpu.make_async_copy(
            right_ref.at[pl.ds(s * bk, bk), pl.ds(column, width)], resid.at[s], load_sem.at[2 * chunks + s]
        )
        for s in range(slots)
    ]
    load_window = [
        pltpu.make_async_copy(
            window_ref.at[:, pl.ds(k * bk, bk)], window.at[k], load_sem.at[2 * chunks + slots + k]
        )
        for k in range(STEPS)
    ]
    for copy in load_x + load_factor + load_right + load_window:
        copy.start()

    pl.semaphore_wait(barrier, rows - 1 + cols - 1)

    def own_send(way, q):
        return pltpu.make_async_remote_copy(
            src_ref=solution_ref.at[pl.ds(q * depth, depth)],
            dst_ref=xs.at[z, q],
            send_sem=gather_send.at[way, z, q],
            recv_sem=gather_recv.at[z, q],
            device_id={"row": lax.rem(z + 1 - 2 * way + rows, rows)},
            device_id_type=MESH,
        )

    def pass_on(way, s, q):
        return pltpu.make_async_remote_copy(
            src_ref=xs.at[s, q],
            dst_ref=xs.at[s, q],
            send_sem=gather_send.at[way, s, q],
            recv_sem=gather_recv.at[s, q],
            device_id={"row": lax.rem(z + 1 - 2 * way + rows, rows)},
            device_id_type=MESH,
        )

    def has_next(way):
        ahead = z + 1 - 2 * way
        return jnp.logical_and(ahead >= 0, ahead < rows)

    for q in range(chunks):
        for way in (0, 1):
            @pl.when(has_next(way))
            def _():
                own_send(way, q).start()

    def send_part(s, slot):
        return pltpu.make_async_remote_copy(
            src_ref=parts.at[s, slot],
            dst_ref=arrived.at[c, slot],
            send_sem=part_send.at[s, slot],
            recv_sem=part_recv.at[c, slot],
            device_id={"col": s},
            device_id_type=MESH,
        )

    def push(s):
        @pl.when(s != c)
        def _():
            for slot in range(slots):
                send_part(s, slot).start()

    def multiply(s, q):
        value = dot3(factor_high[q], factor_low[q], xs[s, q]).reshape(slots, bk, width)

        @pl.when(q == 0)
        def _():
            parts[s] = value

        @pl.when(q > 0)
        def _():
            parts[s] += value

    for q in range(chunks):
        load_factor[q].wait()
        load_x[q].wait()

    def own_chunk(q, carry):
        high, low = halves(factor[q])
        factor_high[q] = high
        factor_low[q] = low
        multiply(z, q)
        return carry

    lax.fori_loop(0, chunks, own_chunk, 0)
    push(z)

    for copy in load_window:
        copy.wait()

    def split_window(k, carry):
        for s in range(slots):
            high, low = halves(window[k, pl.ds(s * bk, bk)])
            window_high[k, s] = high
            window_low[k, s] = low
        return carry

    lax.fori_loop(0, STEPS, split_window, 0)

    def take(t, carry):
        distance = t // (2 * chunks) + 1
        q = lax.rem(t // 2, chunks)
        way = lax.rem(t, 2)
        s = z - distance + 2 * way * distance

        @pl.when(jnp.logical_and(s >= 0, s < rows))
        def _():
            pass_on(way, s, q).wait_recv()

            @pl.when(has_next(way))
            def _():
                pass_on(way, s, q).start()

            multiply(s, q)

            @pl.when(q == chunks - 1)
            def _():
                push(s)

        return carry

    lax.fori_loop(0, (rows - 1) * chunks * 2, take, 0)

    for s in range(slots):
        load_right[s].wait()

    def subtract(slot):
        resid[slot] -= parts[c, slot]
        for i in range(1, cols):
            source = lax.rem(c + i, cols)
            pltpu.make_async_remote_copy(
                src_ref=parts.at[c, slot],
                dst_ref=arrived.at[source, slot],
                send_sem=part_send.at[c, slot],
                recv_sem=part_recv.at[source, slot],
                device_id={"col": source},
                device_id_type=MESH,
            ).wait_recv()
            resid[slot] -= arrived[source, slot]

    def send_solved(k, i):
        return pltpu.make_async_remote_copy(
            src_ref=solved.at[k],
            dst_ref=solved.at[k],
            send_sem=solved_send.at[k, i],
            recv_sem=solved_recv.at[k],
            device_id={"row": lax.rem(k + i, rows)},
            device_id_type=MESH,
        )

    def needs(k, index):
        return last_slot * rows + index > k

    def solve(k, slot):
        root = lax.rem(k, rows)

        @pl.when(z == root)
        def _():
            value = dot3(window_high[k, slot], window_low[k, slot], resid[slot])
            solved[k] = value
            resid[slot] = value
            for i in range(1, rows):
                @pl.when(needs(k, lax.rem(root + i, rows)))
                def _():
                    send_solved(k, i).start()

    def take_solved(k):
        root = lax.rem(k, rows)

        @pl.when(jnp.logical_and(z != root, needs(k, z)))
        def _():
            pltpu.make_async_remote_copy(
                src_ref=solved.at[k],
                dst_ref=solved.at[k],
                send_sem=solved_send.at[k, 0],
                recv_sem=solved_recv.at[k],
                device_id={"row": root},
                device_id_type=MESH,
            ).wait_recv()

    def update(k, slot):
        @pl.when(slot * rows + z > k)
        def _():
            resid[slot] -= dot3(window_high[k, slot], window_low[k, slot], solved[k])

    subtract(0)

    def first(k, carry):
        solve(k, 0)

        @pl.when(k == 0)
        def _():
            subtract(1)

        @pl.when(k > 0)
        def _():
            update(k - 1, 1)

        take_solved(k)
        update(k, 0)
        return carry

    lax.fori_loop(0, rows, first, 0)
    update(rows - 1, 1)

    def second(k, carry):
        solve(k, 1)
        take_solved(k)
        update(k, 1)
        return carry

    lax.fori_loop(rows, STEPS, second, 0)

    for slot in range(slots):
        out_ref[pl.ds(slot * bk, bk)] = resid[slot]

    for q in range(chunks):
        for way in (0, 1):
            @pl.when(has_next(way))
            def _():
                own_send(way, q).wait_send()

    def sent(t, carry):
        distance = t // (2 * chunks) + 1
        q = lax.rem(t // 2, chunks)
        way = lax.rem(t, 2)
        s = z - distance + 2 * way * distance

        @pl.when(jnp.logical_and(jnp.logical_and(s >= 0, s < rows), has_next(way)))
        def _():
            pass_on(way, s, q).wait_send()

        return carry

    lax.fori_loop(0, (rows - 1) * chunks * 2, sent, 0)

    for i in range(1, cols):
        for slot in range(slots):
            send_part(lax.rem(c + i, cols), slot).wait_send()

    def solved_sent(k, carry):
        root = lax.rem(k, rows)

        @pl.when(z == root)
        def _():
            for i in range(1, rows):
                @pl.when(needs(k, lax.rem(root + i, rows)))
                def _():
                    send_solved(k, i).wait_send()

        return carry

    lax.fori_loop(0, STEPS, solved_sent, 0)


def kernel_body(rows, cols, right_side, prev_factor, prev_solution, window_factor):
    bk = window_factor.shape[1] // STEPS
    slots = right_side.shape[0] // bk
    width = right_side.shape[1] // cols
    chunks = 4
    depth = prev_factor.shape[1] // chunks
    height = slots * bk
    f32, bf16 = jnp.float32, jnp.bfloat16
    return pl.pallas_call(
        functools.partial(kernel, rows, cols, slots, bk, chunks, width),
        out_shape=jax.ShapeDtypeStruct((height, width), f32),
        in_specs=[pl.BlockSpec(memory_space=pl.ANY)] * 4,
        out_specs=pl.BlockSpec(memory_space=pltpu.VMEM),
        scratch_shapes=[
            pltpu.VMEM((chunks, height, depth), f32),
            pltpu.VMEM((chunks, height, depth), bf16),
            pltpu.VMEM((chunks, height, depth), bf16),
            pltpu.VMEM((STEPS, height, bk), f32),
            pltpu.VMEM((STEPS, slots, bk, bk), bf16),
            pltpu.VMEM((STEPS, slots, bk, bk), bf16),
            pltpu.VMEM((rows, chunks, depth, width), f32),
            pltpu.VMEM((rows, slots, bk, width), f32),
            pltpu.VMEM((cols, slots, bk, width), f32),
            pltpu.VMEM((slots, bk, width), f32),
            pltpu.VMEM((STEPS, bk, width), f32),
            pltpu.SemaphoreType.DMA((2 * chunks + slots + STEPS,)),
            pltpu.SemaphoreType.DMA((2, rows, chunks)),
            pltpu.SemaphoreType.DMA((rows, chunks)),
            pltpu.SemaphoreType.DMA((cols, slots)),
            pltpu.SemaphoreType.DMA((cols, slots)),
            pltpu.SemaphoreType.DMA((STEPS, rows)),
            pltpu.SemaphoreType.DMA((STEPS,)),
        ],
        compiler_params=pltpu.CompilerParams(
            collective_id=0, has_side_effects=True, vmem_limit_bytes=48 * 1024 * 1024
        ),
    )(right_side, prev_factor, prev_solution, window_factor)


def solution(mesh):
    rows, cols, groups = mesh.shape["row"], mesh.shape["col"], mesh.shape["groups"]

    def body(right_side, prev_factor, prev_solution, window_factor):
        bk = window_factor.shape[1] // STEPS
        slots = right_side.shape[0] // bk
        width = right_side.shape[1] // cols
        fits = (
            rows == cols
            and rows > 1
            and slots == 2
            and rows < STEPS <= 2 * rows
            and width % 128 == 0
            and bk % 128 == 0
            and prev_factor.shape[1] % 512 == 0
        )
        if fits:
            return kernel_body(rows, cols, right_side, prev_factor, prev_solution, window_factor)
        return general_body(right_side, prev_factor, prev_solution, window_factor)

    in_specs = (
        P(("groups", "row"), None),
        P(("groups", "row"), "col"),
        P(("groups", "col"), "row"),
        P(("groups", "row"), None),
    )
    out_specs = P(("groups", "row"), "col")
    return jax.shard_map(body, mesh=mesh, in_specs=in_specs, out_specs=out_specs, check_vma=False)
```

time: 416 us -> 86 us (0.21); the launches traced: 411 us -> 85.8 us
  waiting for transfers between devices: 325 us -> 0 us
  Pallas kernels: 0 us -> 81.2 us
  matrix products: 29.8 us -> 0 us
  local copies, waits for them, and re-layouts: 33.1 us -> 4.56 us
  between operations: 13.5 us -> 0.01 us
  other arithmetic: 8.89 us -> 0 us
    psum x7 -> x0, waiting for transfers between devices: 278 us -> none  [the longest x6 249 us: spread(): return lax.psum(jnp.where(mine, array, jnp.zeros_like(array)), axis)]
    pallas_call x0 -> x1, Pallas kernels: none -> 81.2 us  [kernel_body(): pl.pallas_call(functools.partial(kernel, rows, cols, slots, bk, chunks, w...]
    all_gather x1 -> x0, waiting for transfers between devices: 46.3 us -> none  [body(): lax.all_gather(prev_solution, 'row', axis=1, tiled=True)]
    dot_general x8 -> x0, matrix products: 29.8 us -> none  [the longest x6 21.2 us: advance(): jnp.einsum('sij,jn->sin', tiles[:, :, step, :], solved, precision=lax.Pre...]
    unnamed x13 -> x7, local copies, waits for them, and re-layouts: 16.1 us -> 4.56 us
    another operation x6 -> x0, local copies, waits for them, and re-layouts: 8.22 us -> none
    select_n x6 -> x0, other arithmetic: 6.09 us -> none  [spread(): return lax.psum(jnp.where(mine, array, jnp.zeros_like(array)), axis)]
    slice x2 -> x0, local copies, waits for them, and re-layouts: 4.26 us -> none  [the longest x1 2.4 us: advance(): tiles[:, :, step, :]]
  transfers between devices with their start and end apart: 8 -> 0, of which waited for: 8 -> 0; matrix products, arithmetic and copies ran while one was open for 5% -> 0% of each run, Pallas kernels for 0% -> 0%
where the time goes in v1:
time: 86 us; the launch traced here: 85.8 us
  Pallas kernels  81.2 us (94%)
  local copies, waits for them, and re-layouts  4.56 us (5%)
    pallas_call x1, Pallas kernels, kernel_body(): pl.pallas_call(functools.partial(kernel, rows, cols, slots, bk, chunks, w...  81.2 us
    unnamed x7, local copies, waits for them, and re-layouts  4.56 us

profile of v1, /device:TPU:27, one launch (start us, length us, event | category | flops | bytes accessed | tf_op | source)
XLA Modules:
  0.0 85.8 jit_solution(1686287687289278192)
XLA Ops:
  0.0 0.0 copy-start
  0.0 1.6 %copy-done = f32[512,1024]{1,0:T(8,128)S(1)} copy-done((f32[512,1024]{1,0:T(8,128)S(1)}, f32[512,1024]{1,0:T(8,128)}, u32[]{:S(2)}) %copy-start) | copy-done | bytes 2097176
  1.6 0.0 copy-start.1
  1.6 1.2 %copy-done.1 = f32[512,512]{1,0:T(8,128)S(1)} copy-done((f32[512,512]{1,0:T(8,128)S(1)}, f32[512,512]{1,0:T(8,128)}, u32[]{:S(2)}) %copy-start.1) | copy-done | bytes 1048600
  2.8 0.0 copy-start.2
  2.8 1.0 %copy-done.2 = f32[1024,128]{1,0:T(8,128)S(1)} copy-done((f32[1024,128]{1,0:T(8,128)S(1)}, f32[1024,128]{1,0:T(8,128)}, u32[]{:S(2)}) %copy-start.2) | copy-done | bytes 524312
  3.9 81.2 %shard_map.46 = f32[512,128]{1,0:T(8,128)S(1)} custom-call(f32[512,512]{1,0:T(8,128)S(1)} %copy-done.1, f32[512,1024]{1,0:T(8,128)S(1)} %copy-done, f32[1024,128]{1,0:T(8,128)S(1)} %copy-done.2, f32[512,1536]{1,0:T(8,128)} %window_ref.1), custom_call_target="tpu_custom_call" | custom-call | tf_op jit(solution)/shard_map/pallas_call | solution.py:355
  85.1 0.7 copy.6
Async XLA Ops:
  0.0 1.6 %copy-start = (f32[512,1024]{1,0:T(8,128)S(1)}, f32[512,1024]{1,0:T(8,128)}, u32[]{:S(2)}) copy-start(f32[512,1024]{1,0:T(8,128)} %factor_ref.1) | copy-start | bytes 6291460
  1.6 1.2 %copy-start.1 = (f32[512,512]{1,0:T(8,128)S(1)}, f32[512,512]{1,0:T(8,128)}, u32[]{:S(2)}) copy-start(f32[512,512]{1,0:T(8,128)} %right_ref.1) | copy-start | bytes 3145732
  2.8 1.0 %copy-start.2 = (f32[1024,128]{1,0:T(8,128)S(1)}, f32[1024,128]{1,0:T(8,128)}, u32[]{:S(2)}) copy-start(f32[1024,128]{1,0:T(8,128)} %solution_ref.1) | copy-start | bytes 1572868

commit v2 on v1

--- a/solution.py
+++ b/solution.py
@@ -148,7 +148,9 @@
     def push(s):
         @pl.when(s != c)
         def _():
-            for slot in range(slots):
+            send_part(s, 0).start()
+            send_part(s, 0).wait_send()
+            for slot in range(1, slots):
                 send_part(s, slot).start()
 
     def multiply(s, q):
@@ -187,30 +189,6 @@
         return carry
 
     lax.fori_loop(0, STEPS, split_window, 0)
-
-    def take(t, carry):
-        distance = t // (2 * chunks) + 1
-        q = lax.rem(t // 2, chunks)
-        way = lax.rem(t, 2)
-        s = z - distance + 2 * way * distance
-
-        @pl.when(jnp.logical_and(s >= 0, s < rows))
-        def _():
-            pass_on(way, s, q).wait_recv()
-
-            @pl.when(has_next(way))
-            def _():
-                pass_on(way, s, q).start()
-
-            multiply(s, q)
-
-            @pl.when(q == chunks - 1)
-            def _():
-                push(s)
-
-        return carry
-
-    lax.fori_loop(0, (rows - 1) * chunks * 2, take, 0)
 
     for s in range(slots):
         load_right[s].wait()
@@ -229,18 +207,24 @@
             ).wait_recv()
             resid[slot] -= arrived[source, slot]
 
-    def send_solved(k, i):
+    def send_solved(k, dest):
         return pltpu.make_async_remote_copy(
             src_ref=solved.at[k],
             dst_ref=solved.at[k],
-            send_sem=solved_send.at[k, i],
+            send_sem=solved_send.at[k, dest],
             recv_sem=solved_recv.at[k],
-            device_id={"row": lax.rem(k + i, rows)},
+            device_id={"row": dest},
             device_id_type=MESH,
         )
 
     def needs(k, index):
         return last_slot * rows + index > k
+
+    def sends(k, dest):
+        root = lax.rem(k, rows)
+        straight = jnp.logical_and(z == root, jnp.logical_or(dest < root, k == STEPS - 1))
+        chain = jnp.logical_and(jnp.logical_and(z >= root, dest == z + 1), k < STEPS - 1)
+        return jnp.logical_and(jnp.logical_or(straight, chain), needs(k, dest))
 
     def solve(k, slot):
         root = lax.rem(k, rows)
@@ -250,10 +234,26 @@
             value = dot3(window_high[k, slot], window_low[k, slot], resid[slot])
             solved[k] = value
             resid[slot] = value
-            for i in range(1, rows):
-                @pl.when(needs(k, lax.rem(root + i, rows)))
+
+            @pl.when(jnp.logical_and(root < rows - 1, k < STEPS - 1))
+            def _():
+                send_solved(k, root + 1).start()
+
+            @pl.when(k == STEPS - 1)
+            def _():
+                for back in range(1, rows):
+                    @pl.when(rows - back > root)
+                    def _():
+                        send_solved(k, rows - back).start()
+
+            for dest in range(rows - 1):
+                @pl.when(jnp.logical_and(dest < root, needs(k, dest)))
                 def _():
-                    send_solved(k, i).start()
+                    send_solved(k, dest).start()
+
+                    @pl.when(jnp.logical_and(root == rows - 1, dest == 0))
+                    def _():
+                        send_solved(k, dest).wait_send()
 
     def take_solved(k):
         root = lax.rem(k, rows)
@@ -263,29 +263,66 @@
             pltpu.make_async_remote_copy(
                 src_ref=solved.at[k],
                 dst_ref=solved.at[k],
-                send_sem=solved_send.at[k, 0],
+                send_sem=solved_send.at[k, root],
                 recv_sem=solved_recv.at[k],
                 device_id={"row": root},
                 device_id_type=MESH,
             ).wait_recv()
 
+            @pl.when(jnp.logical_and(jnp.logical_and(z > root, z < rows - 1), k < STEPS - 1))
+            def _():
+                send_solved(k, z + 1).start()
+
     def update(k, slot):
         @pl.when(slot * rows + z > k)
         def _():
             resid[slot] -= dot3(window_high[k, slot], window_low[k, slot], solved[k])
 
-    subtract(0)
+    def take(t, carry):
+        distance = t // (2 * chunks) + 1
+        q = lax.rem(t // 2, chunks)
+        way = lax.rem(t, 2)
+        s = z - distance + 2 * way * distance
+
+        @pl.when(jnp.logical_and(s >= 0, s < rows))
+        def _():
+            pass_on(way, s, q).wait_recv()
+
+            @pl.when(has_next(way))
+            def _():
+                pass_on(way, s, q).start()
+
+            multiply(s, q)
+
+            @pl.when(q == chunks - 1)
+            def _():
+                push(s)
+
+        @pl.when((z == 0) & (c == distance - 1) & (q == 1) & (way == 0))
+        def _():
+            subtract(0)
+            solve(0, 0)
+
+        return carry
+
+    lax.fori_loop(0, rows * chunks * 2, take, 0)
+
+    @pl.when(z > 0)
+    def _():
+        subtract(0)
 
     def first(k, carry):
-        solve(k, 0)
-
-        @pl.when(k == 0)
+        @pl.when(k > 0)
+        def _():
+            solve(k, 0)
+
+        @pl.when(k > 0)
+        def _():
+            update(k - 1, 1)
+
+        @pl.when(k == rows - 1)
         def _():
             subtract(1)
-
-        @pl.when(k > 0)
-        def _():
-            update(k - 1, 1)
 
         take_solved(k)
         update(k, 0)
@@ -326,18 +363,15 @@
     lax.fori_loop(0, (rows - 1) * chunks * 2, sent, 0)
 
     for i in range(1, cols):
-        for slot in range(slots):
+        for slot in range(1, slots):
             send_part(lax.rem(c + i, cols), slot).wait_send()
 
     def solved_sent(k, carry):
-        root = lax.rem(k, rows)
-
-        @pl.when(z == root)
-        def _():
-            for i in range(1, rows):
-                @pl.when(needs(k, lax.rem(root + i, rows)))
-                def _():
-                    send_solved(k, i).wait_send()
+        waited = jnp.logical_and(z == rows - 1, lax.rem(k, rows) == rows - 1)
+        for dest in range(rows):
+            @pl.when(sends(k, dest) & (z != dest) & jnp.logical_not(waited & (dest == 0)))
+            def _():
+                send_solved(k, dest).wait_send()
 
         return carry
 
@@ -378,7 +412,7 @@
             pltpu.SemaphoreType.DMA((STEPS,)),
         ],
         compiler_params=pltpu.CompilerParams(
-            collective_id=0, has_side_effects=True, vmem_limit_bytes=48 * 1024 * 1024
+            collective_id=0, has_side_effects=True, vmem_limit_bytes=62 * 1024 * 1024
         ),
     )(right_side, prev_factor, prev_solution, window_factor)
 

time: 86 us -> 76.5 us (0.89)
  Pallas kernels: 81.2 us -> 74.7 us
  local copies, waits for them, and re-layouts: 4.56 us -> 1.67 us
    pallas_call x1, Pallas kernels: 81.2 us -> 74.7 us  [kernel_body(): pl.pallas_call(functools.partial(kernel, rows, cols, slots, bk, chunks, w...]
    unnamed x7 -> x1, local copies, waits for them, and re-layouts: 4.56 us -> 1.67 us
where the time goes in v2:
time: 76.5 us; the launch traced here: 76.4 us
  Pallas kernels  74.7 us (98%)
  local copies, waits for them, and re-layouts  1.67 us (2%)
    pallas_call x1, Pallas kernels, kernel_body(): pl.pallas_call(functools.partial(kernel, rows, cols, slots, bk, chunks, w...  74.7 us
    unnamed x1, local copies, waits for them, and re-layouts  1.67 us

profile of v2, /device:TPU:27, one launch (start us, length us, event | category | flops | bytes accessed | tf_op | source)
XLA Modules:
  0.0 76.4 jit_solution(12862187992757115610)
XLA Ops:
  0.0 74.7 %shard_map.46 = f32[512,128]{1,0:T(8,128)} custom-call(f32[512,512]{1,0:T(8,128)} %right_ref.1, f32[512,1024]{1,0:T(8,128)} %factor_ref.1, f32[1024,128]{1,0:T(8,128)} %solution_ref.1, f32[512,1536]{1,0:T(8,128)} %window_ref.1), custom_call_target="tpu_custom_call" | custom-call | tf_op jit(solution)/shard_map/pallas_call | solution.py:389
  74.7 1.7 %copy.6 = f32[512,128]{1,0:T(8,128)} copy(f32[512,128]{1,0:T(8,128)} %shard_map.46) | data formatting | bytes 524288

commit v3 on v2

--- a/solution.py
+++ b/solution.py
@@ -63,13 +63,14 @@
     rows, cols, slots, bk, chunks, width,
     right_ref, factor_ref, solution_ref, window_ref, out_ref,
     factor, factor_high, factor_low, window, window_high, window_low,
-    xs, parts, arrived, resid, solved,
+    product_high, product_low, xs, parts, arrived, resid, solved, held,
     load_sem, gather_send, gather_recv, part_send, part_recv, solved_send, solved_recv,
 ):
     z = lax.axis_index("row")
     c = lax.axis_index("col")
     depth = xs.shape[2]
     last_slot = slots - 1
+    hb = bk // 2
 
     barrier = pltpu.get_barrier_semaphore()
     for i in range(1, rows):
@@ -145,10 +146,14 @@
             device_id_type=MESH,
         )
 
-    def push(s):
+    def push(s, slot):
         @pl.when(s != c)
         def _():
-            send_part(s, 0).start()
+            send_part(s, slot).start()
+
+    def push_later(s):
+        @pl.when(s != c)
+        def _():
             send_part(s, 0).wait_send()
             for slot in range(1, slots):
                 send_part(s, slot).start()
@@ -176,19 +181,26 @@
         return carry
 
     lax.fori_loop(0, chunks, own_chunk, 0)
-    push(z)
+    push(z, 0)
 
     for copy in load_window:
         copy.wait()
 
-    def split_window(k, carry):
+    def split_window(k):
         for s in range(slots):
             high, low = halves(window[k, pl.ds(s * bk, bk)])
             window_high[k, s] = high
             window_low[k, s] = low
-        return carry
-
-    lax.fori_loop(0, STEPS, split_window, 0)
+
+    def make_product(slot):
+        k = slot * rows + z
+
+        @pl.when(jnp.logical_and(k > 0, k < STEPS))
+        def _():
+            tile = window[k - 1, pl.ds(slot * bk, bk)]
+            high, low = halves(dot3(window_high[k, slot], window_low[k, slot], tile))
+            product_high[slot] = high
+            product_low[slot] = low
 
     for s in range(slots):
         load_right[s].wait()
@@ -207,12 +219,12 @@
             ).wait_recv()
             resid[slot] -= arrived[source, slot]
 
-    def send_solved(k, dest):
+    def send_solved(k, h, dest):
         return pltpu.make_async_remote_copy(
-            src_ref=solved.at[k],
-            dst_ref=solved.at[k],
-            send_sem=solved_send.at[k, dest],
-            recv_sem=solved_recv.at[k],
+            src_ref=solved.at[k, h],
+            dst_ref=solved.at[k, h],
+            send_sem=solved_send.at[k, h, dest],
+            recv_sem=solved_recv.at[k, h],
             device_id={"row": dest},
             device_id_type=MESH,
         )
@@ -220,63 +232,77 @@
     def needs(k, index):
         return last_slot * rows + index > k
 
-    def sends(k, dest):
+    def first_dest(k, root):
+        return jnp.where(root == rows - 1, 0, jnp.where(k == STEPS - 1, rows - 1, root + 1))
+
+    def far(k, root):
+        return jnp.logical_or(root == rows - 1, k == STEPS - 1)
+
+    def take_solved(k, h):
         root = lax.rem(k, rows)
-        straight = jnp.logical_and(z == root, jnp.logical_or(dest < root, k == STEPS - 1))
-        chain = jnp.logical_and(jnp.logical_and(z >= root, dest == z + 1), k < STEPS - 1)
-        return jnp.logical_and(jnp.logical_or(straight, chain), needs(k, dest))
+        pltpu.make_async_remote_copy(
+            src_ref=solved.at[k, h],
+            dst_ref=solved.at[k, h],
+            send_sem=solved_send.at[k, h, root],
+            recv_sem=solved_recv.at[k, h],
+            device_id={"row": root},
+            device_id_type=MESH,
+        ).wait_recv()
+
+        @pl.when(jnp.logical_and(jnp.logical_and(z > root, z < rows - 1), k < STEPS - 1))
+        def _():
+            send_solved(k, h, z + 1).start()
 
     def solve(k, slot):
         root = lax.rem(k, rows)
-
-        @pl.when(z == root)
-        def _():
-            value = dot3(window_high[k, slot], window_low[k, slot], resid[slot])
-            solved[k] = value
-            resid[slot] = value
-
-            @pl.when(jnp.logical_and(root < rows - 1, k < STEPS - 1))
-            def _():
-                send_solved(k, root + 1).start()
-
-            @pl.when(k == STEPS - 1)
-            def _():
-                for back in range(1, rows):
-                    @pl.when(rows - back > root)
-                    def _():
-                        send_solved(k, rows - back).start()
-
-            for dest in range(rows - 1):
-                @pl.when(jnp.logical_and(dest < root, needs(k, dest)))
-                def _():
-                    send_solved(k, dest).start()
-
-                    @pl.when(jnp.logical_and(root == rows - 1, dest == 0))
-                    def _():
-                        send_solved(k, dest).wait_send()
-
-    def take_solved(k):
-        root = lax.rem(k, rows)
-
-        @pl.when(jnp.logical_and(z != root, needs(k, z)))
-        def _():
-            pltpu.make_async_remote_copy(
-                src_ref=solved.at[k],
-                dst_ref=solved.at[k],
-                send_sem=solved_send.at[k, root],
-                recv_sem=solved_recv.at[k],
-                device_id={"row": root},
-                device_id_type=MESH,
-            ).wait_recv()
-
-            @pl.when(jnp.logical_and(jnp.logical_and(z > root, z < rows - 1), k < STEPS - 1))
-            def _():
-                send_solved(k, z + 1).start()
+        for h in range(2):
+            span = pl.ds(h * hb, hb)
+            held[h] = dot3(window_high[k, slot, span], window_low[k, slot, span], resid[slot])
+
+        @pl.when(k > 0)
+        def _():
+            take_solved(k - 1, 0)
+            for h in range(2):
+                span = pl.ds(h * hb, hb)
+                held[h] -= dot3(
+                    product_high[slot, span, 0:hb], product_low[slot, span, 0:hb], solved[k - 1, 0]
+                )
+            take_solved(k - 1, 1)
+
+        for h in range(2):
+            span = pl.ds(h * hb, hb)
+
+            @pl.when(k > 0)
+            def _():
+                held[h] -= dot3(
+                    product_high[slot, span, hb:bk], product_low[slot, span, hb:bk], solved[k - 1, 1]
+                )
+
+            solved[k, h] = held[h]
+            send_solved(k, h, first_dest(k, root)).start()
+        for h in range(2):
+            resid[slot, pl.ds(h * hb, hb)] = held[h]
+
+        @pl.when(far(k, root))
+        def _():
+            for h in range(2):
+                send_solved(k, h, first_dest(k, root)).wait_send()
+
+        for dest in range(rows):
+            @pl.when(others(k, root, dest))
+            def _():
+                for h in range(2):
+                    send_solved(k, h, dest).start()
+
+    def others(k, root, dest):
+        side = (dest < root) | ((dest > root) & (k == STEPS - 1))
+        return side & (first_dest(k, root) != dest) & needs(k, dest)
 
     def update(k, slot):
         @pl.when(slot * rows + z > k)
         def _():
-            resid[slot] -= dot3(window_high[k, slot], window_low[k, slot], solved[k])
+            block = solved[k].reshape(bk, width)
+            resid[slot] -= dot3(window_high[k, slot], window_low[k, slot], block)
 
     def take(t, carry):
         distance = t // (2 * chunks) + 1
@@ -296,9 +322,25 @@
 
             @pl.when(q == chunks - 1)
             def _():
-                push(s)
-
-        @pl.when((z == 0) & (c == distance - 1) & (q == 1) & (way == 0))
+                push(s, 0)
+
+        @pl.when(t < STEPS)
+        def _():
+            split_window(t)
+
+        for slot in range(slots):
+            @pl.when(t == STEPS + slot)
+            def _():
+                make_product(slot)
+
+        before = s + (1 - 2 * way)
+        twice = (distance == 1) & (way == 1)
+
+        @pl.when((q == 1) & (before >= 0) & (before < rows) & jnp.logical_not(twice))
+        def _():
+            push_later(before)
+
+        @pl.when((z == 0) & (c == distance - 1) & (q == 2) & (way == 0))
         def _():
             subtract(0)
             solve(0, 0)
@@ -311,33 +353,41 @@
     def _():
         subtract(0)
 
-    def first(k, carry):
-        @pl.when(k > 0)
-        def _():
-            solve(k, 0)
-
-        @pl.when(k > 0)
+    def step(k, carry):
+        root = lax.rem(k, rows)
+        is_root = z == root
+        is_next = jnp.logical_and(z == lax.rem(k + 1, rows), k + 1 < STEPS)
+
+        @pl.when(is_root)
+        def _():
+            @pl.when(k > 0)
+            def _():
+                solve(k, k // rows)
+
+        @pl.when(jnp.logical_and(needs(k, z), jnp.logical_not(is_root | is_next)))
+        def _():
+            for h in range(2):
+                take_solved(k, h)
+
+        @pl.when(jnp.logical_not(is_root | is_next))
+        def _():
+            update(k, 0)
+
+        @pl.when(jnp.logical_and(is_root, (k > 0) & (k < rows)))
         def _():
             update(k - 1, 1)
 
+        @pl.when(jnp.logical_or(jnp.logical_not(is_root | is_next), is_root & (k < rows)))
+        def _():
+            update(k, 1)
+
         @pl.when(k == rows - 1)
         def _():
             subtract(1)
 
-        take_solved(k)
-        update(k, 0)
         return carry
 
-    lax.fori_loop(0, rows, first, 0)
-    update(rows - 1, 1)
-
-    def second(k, carry):
-        solve(k, 1)
-        take_solved(k)
-        update(k, 1)
-        return carry
-
-    lax.fori_loop(rows, STEPS, second, 0)
+    lax.fori_loop(0, STEPS, step, 0)
 
     for slot in range(slots):
         out_ref[pl.ds(slot * bk, bk)] = resid[slot]
@@ -367,11 +417,16 @@
             send_part(lax.rem(c + i, cols), slot).wait_send()
 
     def solved_sent(k, carry):
-        waited = jnp.logical_and(z == rows - 1, lax.rem(k, rows) == rows - 1)
+        root = lax.rem(k, rows)
+        start = (z == root) & jnp.logical_not(far(k, root))
+        middle = (z > root) & (z < rows - 1) & (k < STEPS - 1)
         for dest in range(rows):
-            @pl.when(sends(k, dest) & (z != dest) & jnp.logical_not(waited & (dest == 0)))
-            def _():
-                send_solved(k, dest).wait_send()
+            near = (start & (first_dest(k, root) == dest)) | (middle & (dest == z + 1))
+
+            @pl.when((near | ((z == root) & others(k, root, dest))) & (z != dest))
+            def _():
+                for h in range(2):
+                    send_solved(k, h, dest).wait_send()
 
         return carry
 
@@ -398,18 +453,21 @@
             pltpu.VMEM((STEPS, height, bk), f32),
             pltpu.VMEM((STEPS, slots, bk, bk), bf16),
             pltpu.VMEM((STEPS, slots, bk, bk), bf16),
+            pltpu.VMEM((slots, bk, bk), bf16),
+            pltpu.VMEM((slots, bk, bk), bf16),
             pltpu.VMEM((rows, chunks, depth, width), f32),
             pltpu.VMEM((rows, slots, bk, width), f32),
             pltpu.VMEM((cols, slots, bk, width), f32),
             pltpu.VMEM((slots, bk, width), f32),
-            pltpu.VMEM((STEPS, bk, width), f32),
+            pltpu.VMEM((STEPS, 2, bk // 2, width), f32),
+            pltpu.VMEM((2, bk // 2, width), f32),
             pltpu.SemaphoreType.DMA((2 * chunks + slots + STEPS,)),
             pltpu.SemaphoreType.DMA((2, rows, chunks)),
             pltpu.SemaphoreType.DMA((rows, chunks)),
             pltpu.SemaphoreType.DMA((cols, slots)),
             pltpu.SemaphoreType.DMA((cols, slots)),
-            pltpu.SemaphoreType.DMA((STEPS, rows)),
-            pltpu.SemaphoreType.DMA((STEPS,)),
+            pltpu.SemaphoreType.DMA((STEPS, 2, rows)),
+            pltpu.SemaphoreType.DMA((STEPS, 2)),
         ],
         compiler_params=pltpu.CompilerParams(
             collective_id=0, has_side_effects=True, vmem_limit_bytes=62 * 1024 * 1024
@@ -428,9 +486,9 @@
             rows == cols
             and rows > 1
             and slots == 2
-            and rows < STEPS <= 2 * rows
+            and rows < STEPS < 2 * rows
             and width % 128 == 0
-            and bk % 128 == 0
+            and bk % 256 == 0
             and prev_factor.shape[1] % 512 == 0
         )
         if fits:

time: 76.5 us -> 74.6 us (0.975)
  Pallas kernels: 74.7 us -> 72.5 us
    pallas_call x1, Pallas kernels: 74.7 us -> 72.5 us  [kernel_body(): pl.pallas_call(functools.partial(kernel, rows, cols, slots, bk, chunks, w...]
where the time goes in v3:
time: 74.6 us; the launch traced here: 74.2 us
  Pallas kernels  72.5 us (97%)
  local copies, waits for them, and re-layouts  1.67 us (2%)
    pallas_call x1, Pallas kernels, kernel_body(): pl.pallas_call(functools.partial(kernel, rows, cols, slots, bk, chunks, w...  72.5 us
    unnamed x1, local copies, waits for them, and re-layouts  1.67 us

profile of v3, /device:TPU:27, one launch (start us, length us, event | category | flops | bytes accessed | tf_op | source)
XLA Modules:
  0.0 74.2 jit_solution(3898514789162378654)
XLA Ops:
  0.0 72.5 %shard_map.46 = f32[512,128]{1,0:T(8,128)} custom-call(f32[512,512]{1,0:T(8,128)} %right_ref.1, f32[512,1024]{1,0:T(8,128)} %factor_ref.1, f32[1024,128]{1,0:T(8,128)} %solution_ref.1, f32[512,1536]{1,0:T(8,128)} %window_ref.1), custom_call_target="tpu_custom_call" | custom-call | tf_op jit(solution)/shard_map/pallas_call | solution.py:444
  72.5 1.7 %copy.6 = f32[512,128]{1,0:T(8,128)} copy(f32[512,128]{1,0:T(8,128)} %shard_map.46) | data formatting | bytes 524288

commit v4 on v2

--- a/solution.py
+++ b/solution.py
@@ -8,6 +8,7 @@
 from jax.sharding import PartitionSpec as P
 
 STEPS = 6
+HUB = 1
 MESH = pl.DeviceIdType.MESH
 
 
@@ -63,13 +64,15 @@
     rows, cols, slots, bk, chunks, width,
     right_ref, factor_ref, solution_ref, window_ref, out_ref,
     factor, factor_high, factor_low, window, window_high, window_low,
-    xs, parts, arrived, resid, solved,
-    load_sem, gather_send, gather_recv, part_send, part_recv, solved_send, solved_recv,
+    stage, wall_high, wall_low, solved_high, solved_low,
+    xs, parts, arrived, resid, inbox, solved,
+    load_sem, gather_send, gather_recv, part_send, part_recv,
+    tile_send, tile_recv, box_send, box_recv, solved_send, solved_recv,
 ):
     z = lax.axis_index("row")
     c = lax.axis_index("col")
     depth = xs.shape[2]
-    last_slot = slots - 1
+    quarter = bk // cols
 
     barrier = pltpu.get_barrier_semaphore()
     for i in range(1, rows):
@@ -105,6 +108,39 @@
 
     pl.semaphore_wait(barrier, rows - 1 + cols - 1)
 
+    def tile_piece(e, part):
+        return stage.at[e - 2, pl.ds(pl.multiple_of(part * quarter, quarter), quarter), 0 : (e + 1) * bk]
+
+    def send_tiles(e):
+        start = pl.multiple_of((e // rows) * bk + c * quarter, quarter)
+        return pltpu.make_async_remote_copy(
+            src_ref=window_ref.at[pl.ds(start, quarter), 0 : (e + 1) * bk],
+            dst_ref=tile_piece(e, c),
+            send_sem=tile_send.at[e - 2, c, 0],
+            recv_sem=tile_recv.at[e - 2, c],
+            device_id={"row": HUB},
+            device_id_type=MESH,
+        )
+
+    def share_tiles(e, part, i, dest):
+        return pltpu.make_async_remote_copy(
+            src_ref=tile_piece(e, part),
+            dst_ref=tile_piece(e, part),
+            send_sem=tile_send.at[e - 2, part, i],
+            recv_sem=tile_recv.at[e - 2, part],
+            device_id={"col": dest},
+            device_id_type=MESH,
+        )
+
+    far_col = lax.rem(c + 2, cols)
+    near_col = c + 1 - 2 * lax.rem(c, 2)
+    near_far_col = lax.rem(near_col + 2, cols)
+
+    for e in (2, 3, 4):
+        @pl.when(z == e % rows)
+        def _():
+            send_tiles(e).start()
+
     def own_send(way, q):
         return pltpu.make_async_remote_copy(
             src_ref=solution_ref.at[pl.ds(q * depth, depth)],
@@ -145,10 +181,14 @@
             device_id_type=MESH,
         )
 
-    def push(s):
+    def push(s, slot):
         @pl.when(s != c)
         def _():
-            send_part(s, 0).start()
+            send_part(s, slot).start()
+
+    def push_later(s):
+        @pl.when(s != c)
+        def _():
             send_part(s, 0).wait_send()
             for slot in range(1, slots):
                 send_part(s, slot).start()
@@ -176,19 +216,16 @@
         return carry
 
     lax.fori_loop(0, chunks, own_chunk, 0)
-    push(z)
+    push(z, 0)
 
     for copy in load_window:
         copy.wait()
 
-    def split_window(k, carry):
+    def split_window(k):
         for s in range(slots):
             high, low = halves(window[k, pl.ds(s * bk, bk)])
             window_high[k, s] = high
             window_low[k, s] = low
-        return carry
-
-    lax.fori_loop(0, STEPS, split_window, 0)
 
     for s in range(slots):
         load_right[s].wait()
@@ -207,76 +244,94 @@
             ).wait_recv()
             resid[slot] -= arrived[source, slot]
 
-    def send_solved(k, dest):
+    def send_box(e, slot):
+        return pltpu.make_async_remote_copy(
+            src_ref=resid.at[slot],
+            dst_ref=inbox.at[e - 2],
+            send_sem=box_send.at[e - 2],
+            recv_sem=box_recv.at[e - 2],
+            device_id={"row": HUB},
+            device_id_type=MESH,
+        )
+
+    def send_solved(k, i, dest):
         return pltpu.make_async_remote_copy(
             src_ref=solved.at[k],
             dst_ref=solved.at[k],
-            send_sem=solved_send.at[k, dest],
+            send_sem=solved_send.at[k, i],
             recv_sem=solved_recv.at[k],
             device_id={"row": dest},
             device_id_type=MESH,
         )
 
-    def needs(k, index):
-        return last_slot * rows + index > k
-
-    def sends(k, dest):
-        root = lax.rem(k, rows)
-        straight = jnp.logical_and(z == root, jnp.logical_or(dest < root, k == STEPS - 1))
-        chain = jnp.logical_and(jnp.logical_and(z >= root, dest == z + 1), k < STEPS - 1)
-        return jnp.logical_and(jnp.logical_or(straight, chain), needs(k, dest))
-
-    def solve(k, slot):
-        root = lax.rem(k, rows)
-
-        @pl.when(z == root)
-        def _():
-            value = dot3(window_high[k, slot], window_low[k, slot], resid[slot])
-            solved[k] = value
-            resid[slot] = value
-
-            @pl.when(jnp.logical_and(root < rows - 1, k < STEPS - 1))
-            def _():
-                send_solved(k, root + 1).start()
-
-            @pl.when(k == STEPS - 1)
-            def _():
-                for back in range(1, rows):
-                    @pl.when(rows - back > root)
-                    def _():
-                        send_solved(k, rows - back).start()
-
-            for dest in range(rows - 1):
-                @pl.when(jnp.logical_and(dest < root, needs(k, dest)))
-                def _():
-                    send_solved(k, dest).start()
-
-                    @pl.when(jnp.logical_and(root == rows - 1, dest == 0))
-                    def _():
-                        send_solved(k, dest).wait_send()
-
-    def take_solved(k):
-        root = lax.rem(k, rows)
-
-        @pl.when(jnp.logical_and(z != root, needs(k, z)))
-        def _():
-            pltpu.make_async_remote_copy(
-                src_ref=solved.at[k],
-                dst_ref=solved.at[k],
-                send_sem=solved_send.at[k, root],
-                recv_sem=solved_recv.at[k],
-                device_id={"row": root},
-                device_id_type=MESH,
-            ).wait_recv()
-
-            @pl.when(jnp.logical_and(jnp.logical_and(z > root, z < rows - 1), k < STEPS - 1))
-            def _():
-                send_solved(k, z + 1).start()
-
-    def update(k, slot):
-        @pl.when(slot * rows + z > k)
-        def _():
-            resid[slot] -= dot3(window_high[k, slot], window_low[k, slot], solved[k])
+    def begin():
+        subtract(0)
+
+        @pl.when(z == 0)
+        def _():
+            solved[0] = dot3(window_high[0, 0], window_low[0, 0], resid[0])
+            send_solved(0, 0, HUB).start()
+
+        for e in (2, 3):
+            @pl.when(z == e)
+            def _():
+                send_box(e, 0).start()
+
+    def keep(k):
+        high, low = halves(solved[k])
+        solved_high[pl.ds(k * bk, bk)] = high
+        solved_low[pl.ds(k * bk, bk)] = low
+
+    def hub_tiles():
+        for e in (2, 3, 4):
+            for part in (near_col, near_far_col):
+                share_tiles(e, part, 2, near_col).wait_recv()
+        for e in range(1, STEPS):
+            for k in range(e + 1):
+                span = slice(k * bk, (k + 1) * bk)
+                if e in (1, STEPS - 1):
+                    wall_high[e - 1, :, span] = window_high[k, e // rows]
+                    wall_low[e - 1, :, span] = window_low[k, e // rows]
+                else:
+                    high, low = halves(stage[e - 2, :, span])
+                    wall_high[e - 1, :, span] = high
+                    wall_low[e - 1, :, span] = low
+
+    def hub_solve():
+        send_solved(0, 0, 2).wait_recv()
+        send_solved(0, 0, 2).start()
+        keep(0)
+        dot = functools.partial(jnp.dot, preferred_element_type=jnp.float32)
+        for e in range(1, STEPS):
+            done = e * bk
+            t_high, t_low = wall_high[e - 1, :, 0:done], wall_low[e - 1, :, 0:done]
+            s_high, s_low = solved_high[0:done], solved_low[0:done]
+            total = dot(t_high, s_high) + (dot(t_high, s_low) + dot(t_low, s_high))
+            if e == 1:
+                value = resid[0] - total
+            elif e == STEPS - 1:
+                subtract(1)
+                value = resid[1] - total
+            else:
+                send_box(e, 0).wait_recv()
+                value = inbox[e - 2] - total
+            span = slice(done, done + bk)
+            solved[e] = dot3(wall_high[e - 1, :, span], wall_low[e - 1, :, span], value)
+            send_solved(e, 0, 2).start()
+            if e == 4:
+                send_solved(e, 1, 0).start()
+            if e < STEPS - 1:
+                keep(e)
+
+    def update(k, carry):
+        send_solved(k, 0, HUB).wait_recv()
+
+        @pl.when(z == 2)
+        def _():
+            send_solved(k, 0, 3).start()
+
+        resid[1] -= dot3(window_high[k, 1], window_low[k, 1], solved[k])
+        return carry
 
     def take(t, carry):
         distance = t // (2 * chunks) + 1
@@ -296,51 +351,63 @@
 
             @pl.when(q == chunks - 1)
             def _():
-                push(s)
-
-        @pl.when((z == 0) & (c == distance - 1) & (q == 1) & (way == 0))
-        def _():
-            subtract(0)
-            solve(0, 0)
+                push(s, 0)
+
+        @pl.when(t < STEPS)
+        def _():
+            split_window(t)
+
+        for e in (2, 4, 3):
+            @pl.when((z == HUB) & (t == (5 if e == 3 else 3)))
+            def _():
+                share_tiles(e, c, 1, far_col).wait_recv()
+                share_tiles(e, c, 1, far_col).start()
+                share_tiles(e, c, 2, near_col).start()
+
+            @pl.when((z == HUB) & (t == 4 * chunks))
+            def _():
+                share_tiles(e, far_col, 2, near_col).wait_recv()
+                share_tiles(e, far_col, 2, near_col).start()
+
+        before = s + (1 - 2 * way)
+        twice = (distance == 1) & (way == 1)
+
+        @pl.when((q == 1) & (before >= 0) & (before < rows) & jnp.logical_not(twice))
+        def _():
+            push_later(before)
+
+        @pl.when((jnp.abs(z - c) == distance - 1) & (q == 2) & (way == 0))
+        def _():
+            begin()
 
         return carry
 
     lax.fori_loop(0, rows * chunks * 2, take, 0)
 
-    @pl.when(z > 0)
+    def write(slot, value):
+        out_ref[pl.ds(slot * bk, bk)] = value
+
+    @pl.when(z == 0)
     def _():
-        subtract(0)
-
-    def first(k, carry):
-        @pl.when(k > 0)
-        def _():
-            solve(k, 0)
-
-        @pl.when(k > 0)
-        def _():
-            update(k - 1, 1)
-
-        @pl.when(k == rows - 1)
-        def _():
-            subtract(1)
-
-        take_solved(k)
-        update(k, 0)
-        return carry
-
-    lax.fori_loop(0, rows, first, 0)
-    update(rows - 1, 1)
-
-    def second(k, carry):
-        solve(k, 1)
-        take_solved(k)
-        update(k, 1)
-        return carry
-
-    lax.fori_loop(rows, STEPS, second, 0)
-
-    for slot in range(slots):
-        out_ref[pl.ds(slot * bk, bk)] = resid[slot]
+        subtract(1)
+        send_box(4, 1).start()
+        write(0, solved[0])
+        send_solved(4, 1, HUB).wait_recv()
+        write(1, solved[4])
+
+    @pl.when(z == HUB)
+    def _():
+        hub_tiles()
+        hub_solve()
+        write(0, solved[1])
+        write(1, solved[STEPS - 1])
+
+    @pl.when(z > HUB)
+    def _():
+        subtract(1)
+        lax.fori_loop(0, STEPS, update, 0)
+        write(0, solved[z])
+        write(1, resid[1])
 
     for q in range(chunks):
         for way in (0, 1):
@@ -366,16 +433,30 @@
         for slot in range(1, slots):
             send_part(lax.rem(c + i, cols), slot).wait_send()
 
-    def solved_sent(k, carry):
-        waited = jnp.logical_and(z == rows - 1, lax.rem(k, rows) == rows - 1)
-        for dest in range(rows):
-            @pl.when(sends(k, dest) & (z != dest) & jnp.logical_not(waited & (dest == 0)))
-            def _():
-                send_solved(k, dest).wait_send()
-
-        return carry
-
-    lax.fori_loop(0, STEPS, solved_sent, 0)
+    for e in (2, 3, 4):
+        @pl.when(z == e % rows)
+        def _():
+            send_tiles(e).wait_send()
+            send_box(e, e // rows).wait_send()
+
+        @pl.when(z == HUB)
+        def _():
+            share_tiles(e, c, 1, far_col).wait_send()
+            share_tiles(e, c, 2, near_col).wait_send()
+            share_tiles(e, far_col, 2, near_col).wait_send()
+
+    @pl.when(z == 0)
+    def _():
+        send_solved(0, 0, HUB).wait_send()
+
+    @pl.when(z == HUB)
+    def _():
+        send_solved(4, 1, 0).wait_send()
+
+    for k in range(STEPS):
+        @pl.when((z == HUB) | (z == 2))
+        def _():
+            send_solved(k, 0, z + 1).wait_send()
 
 
 def kernel_body(rows, cols, right_side, prev_factor, prev_solution, window_factor):
@@ -398,17 +479,27 @@
             pltpu.VMEM((STEPS, height, bk), f32),
             pltpu.VMEM((STEPS, slots, bk, bk), bf16),
             pltpu.VMEM((STEPS, slots, bk, bk), bf16),
+            pltpu.VMEM((3, bk, 5 * bk), f32),
+            pltpu.VMEM((STEPS - 1, bk, STEPS * bk), bf16),
+            pltpu.VMEM((STEPS - 1, bk, STEPS * bk), bf16),
+            pltpu.VMEM((STEPS * bk, width), bf16),
+            pltpu.VMEM((STEPS * bk, width), bf16),
             pltpu.VMEM((rows, chunks, depth, width), f32),
             pltpu.VMEM((rows, slots, bk, width), f32),
             pltpu.VMEM((cols, slots, bk, width), f32),
             pltpu.VMEM((slots, bk, width), f32),
+            pltpu.VMEM((3, bk, width), f32),
             pltpu.VMEM((STEPS, bk, width), f32),
             pltpu.SemaphoreType.DMA((2 * chunks + slots + STEPS,)),
             pltpu.SemaphoreType.DMA((2, rows, chunks)),
             pltpu.SemaphoreType.DMA((rows, chunks)),
             pltpu.SemaphoreType.DMA((cols, slots)),
             pltpu.SemaphoreType.DMA((cols, slots)),
-            pltpu.SemaphoreType.DMA((STEPS, rows)),
+            pltpu.SemaphoreType.DMA((3, cols, 3)),
+            pltpu.SemaphoreType.DMA((3, cols)),
+            pltpu.SemaphoreType.DMA((3,)),
+            pltpu.SemaphoreType.DMA((3,)),
+            pltpu.SemaphoreType.DMA((STEPS, 2)),
             pltpu.SemaphoreType.DMA((STEPS,)),
         ],
         compiler_params=pltpu.CompilerParams(
@@ -425,12 +516,10 @@
         slots = right_side.shape[0] // bk
         width = right_side.shape[1] // cols
         fits = (
-            rows == cols
-            and rows > 1
+            rows == cols == 4
             and slots == 2
-            and rows < STEPS <= 2 * rows
             and width % 128 == 0
-            and bk % 128 == 0
+            and bk % 256 == 0
             and prev_factor.shape[1] % 512 == 0
         )
         if fits:

time: 76.5 us -> 79.1 us (1.034)
  Pallas kernels: 74.7 us -> 77.3 us
    pallas_call x1, Pallas kernels: 74.7 us -> 77.3 us  [kernel_body(): pl.pallas_call(functools.partial(kernel, rows, cols, slots, bk, chunks, w...]
where the time goes in v4:
time: 79.1 us; the launch traced here: 79 us
  Pallas kernels  77.3 us (98%)
  local copies, waits for them, and re-layouts  1.67 us (2%)
    pallas_call x1, Pallas kernels, kernel_body(): pl.pallas_call(functools.partial(kernel, rows, cols, slots, bk, chunks, w...  77.3 us
    unnamed x1, local copies, waits for them, and re-layouts  1.67 us

profile of v4, /device:TPU:27, one launch (start us, length us, event | category | flops | bytes accessed | tf_op | source)
XLA Modules:
  0.0 79.0 jit_solution(2415194877176431651)
XLA Ops:
  0.0 77.3 %shard_map.46 = f32[512,128]{1,0:T(8,128)} custom-call(f32[512,512]{1,0:T(8,128)} %right_ref.1, f32[512,1024]{1,0:T(8,128)} %factor_ref.1, f32[1024,128]{1,0:T(8,128)} %solution_ref.1, f32[512,1536]{1,0:T(8,128)} %window_ref.1), custom_call_target="tpu_custom_call" | custom-call | tf_op jit(solution)/shard_map/pallas_call | solution.py:470
  77.3 1.7 %copy.6 = f32[512,128]{1,0:T(8,128)} copy(f32[512,128]{1,0:T(8,128)} %shard_map.46) | data formatting | bytes 524288

commit v5 on v3

--- a/solution.py
+++ b/solution.py
@@ -53,17 +53,21 @@
     return high, low
 
 
-def dot3(a_high, a_low, b):
-    b_high, b_low = halves(b)
-    dot = functools.partial(jnp.dot, preferred_element_type=jnp.float32)
-    return dot(a_high, b_high) + (dot(a_high, b_low) + dot(a_low, b_high))
+def triple(value):
+    high, low = halves(value)
+    return jnp.concatenate([high, high, low], axis=1)
+
+
+def dot3(a3, b):
+    high, low = halves(b)
+    b3 = jnp.concatenate([high, low, high], axis=0)
+    return jnp.dot(a3, b3, preferred_element_type=jnp.float32)
 
 
 def kernel(
     rows, cols, slots, bk, chunks, width,
     right_ref, factor_ref, solution_ref, window_ref, out_ref,
-    factor, factor_high, factor_low, window, window_high, window_low,
-    product_high, product_low, xs, parts, arrived, resid, solved, held,
+    factor, factor3, window, window3, product3, xs, parts, arrived, resid, solved, held,
     load_sem, gather_send, gather_recv, part_send, part_recv, solved_send, solved_recv,
 ):
     z = lax.axis_index("row")
@@ -159,7 +163,7 @@
                 send_part(s, slot).start()
 
     def multiply(s, q):
-        value = dot3(factor_high[q], factor_low[q], xs[s, q]).reshape(slots, bk, width)
+        value = dot3(factor3[q], xs[s, q]).reshape(slots, bk, width)
 
         @pl.when(q == 0)
         def _():
@@ -174,9 +178,7 @@
         load_x[q].wait()
 
     def own_chunk(q, carry):
-        high, low = halves(factor[q])
-        factor_high[q] = high
-        factor_low[q] = low
+        factor3[q] = triple(factor[q])
         multiply(z, q)
         return carry
 
@@ -188,9 +190,7 @@
 
     def split_window(k):
         for s in range(slots):
-            high, low = halves(window[k, pl.ds(s * bk, bk)])
-            window_high[k, s] = high
-            window_low[k, s] = low
+            window3[k, s] = triple(window[k, pl.ds(s * bk, bk)])
 
     def make_product(slot):
         k = slot * rows + z
@@ -198,9 +198,9 @@
         @pl.when(jnp.logical_and(k > 0, k < STEPS))
         def _():
             tile = window[k - 1, pl.ds(slot * bk, bk)]
-            high, low = halves(dot3(window_high[k, slot], window_low[k, slot], tile))
-            product_high[slot] = high
-            product_low[slot] = low
+            value = dot3(window3[k, slot], tile)
+            for j in range(2):
+                product3[slot, j] = triple(value[:, j * hb : (j + 1) * hb])
 
     for s in range(slots):
         load_right[s].wait()
@@ -257,16 +257,14 @@
         root = lax.rem(k, rows)
         for h in range(2):
             span = pl.ds(h * hb, hb)
-            held[h] = dot3(window_high[k, slot, span], window_low[k, slot, span], resid[slot])
+            held[h] = dot3(window3[k, slot, span], resid[slot])
 
         @pl.when(k > 0)
         def _():
             take_solved(k - 1, 0)
             for h in range(2):
                 span = pl.ds(h * hb, hb)
-                held[h] -= dot3(
-                    product_high[slot, span, 0:hb], product_low[slot, span, 0:hb], solved[k - 1, 0]
-                )
+                held[h] -= dot3(product3[slot, 0, span], solved[k - 1, 0])
             take_solved(k - 1, 1)
 
         for h in range(2):
@@ -274,9 +272,7 @@
 
             @pl.when(k > 0)
             def _():
-                held[h] -= dot3(
-                    product_high[slot, span, hb:bk], product_low[slot, span, hb:bk], solved[k - 1, 1]
-                )
+                held[h] -= dot3(product3[slot, 1, span], solved[k - 1, 1])
 
             solved[k, h] = held[h]
             send_solved(k, h, first_dest(k, root)).start()
@@ -302,7 +298,7 @@
         @pl.when(slot * rows + z > k)
         def _():
             block = solved[k].reshape(bk, width)
-            resid[slot] -= dot3(window_high[k, slot], window_low[k, slot], block)
+            resid[slot] -= dot3(window3[k, slot], block)
 
     def take(t, carry):
         distance = t // (2 * chunks) + 1
@@ -448,13 +444,10 @@
         out_specs=pl.BlockSpec(memory_space=pltpu.VMEM),
         scratch_shapes=[
             pltpu.VMEM((chunks, height, depth), f32),
-            pltpu.VMEM((chunks, height, depth), bf16),
-            pltpu.VMEM((chunks, height, depth), bf16),
+            pltpu.VMEM((chunks, height, 3 * depth), bf16),
             pltpu.VMEM((STEPS, height, bk), f32),
-            pltpu.VMEM((STEPS, slots, bk, bk), bf16),
-            pltpu.VMEM((STEPS, slots, bk, bk), bf16),
-            pltpu.VMEM((slots, bk, bk), bf16),
-            pltpu.VMEM((slots, bk, bk), bf16),
+            pltpu.VMEM((STEPS, slots, bk, 3 * bk), bf16),
+            pltpu.VMEM((slots, 2, bk, 3 * (bk // 2)), bf16),
             pltpu.VMEM((rows, chunks, depth, width), f32),
             pltpu.VMEM((rows, slots, bk, width), f32),
             pltpu.VMEM((cols, slots, bk, width), f32),

time: 74.6 us -> 74.6 us (level)
  no operation moved by 1% of the time
where the time goes in v5:
time: 74.6 us; the launch traced here: 74.2 us
  Pallas kernels  72.5 us (97%)
  local copies, waits for them, and re-layouts  1.67 us (2%)
    pallas_call x1, Pallas kernels, kernel_body(): pl.pallas_call(functools.partial(kernel, rows, cols, slots, bk, chunks, w...  72.5 us
    unnamed x1, local copies, waits for them, and re-layouts  1.67 us

profile of v5, /device:TPU:27, one launch (start us, length us, event | category | flops | bytes accessed | tf_op | source)
XLA Modules:
  0.0 74.2 jit_solution(7244936616510817618)
XLA Ops:
  0.0 72.5 %shard_map.46 = f32[512,128]{1,0:T(8,128)} custom-call(f32[512,512]{1,0:T(8,128)} %right_ref.1, f32[512,1024]{1,0:T(8,128)} %factor_ref.1, f32[1024,128]{1,0:T(8,128)} %solution_ref.1, f32[512,1536]{1,0:T(8,128)} %window_ref.1), custom_call_target="tpu_custom_call" | custom-call | tf_op jit(solution)/shard_map/pallas_call | solution.py:440
  72.5 1.7 %copy.6 = f32[512,128]{1,0:T(8,128)} copy(f32[512,128]{1,0:T(8,128)} %shard_map.46) | data formatting | bytes 524288

commit v6 on v5

--- a/solution.py
+++ b/solution.py
@@ -255,16 +255,12 @@
 
     def solve(k, slot):
         root = lax.rem(k, rows)
-        for h in range(2):
-            span = pl.ds(h * hb, hb)
-            held[h] = dot3(window3[k, slot, span], resid[slot])
+        held[...] = dot3(window3[k, slot], resid[slot]).reshape(2, hb, width)
 
         @pl.when(k > 0)
         def _():
             take_solved(k - 1, 0)
-            for h in range(2):
-                span = pl.ds(h * hb, hb)
-                held[h] -= dot3(product3[slot, 0, span], solved[k - 1, 0])
+            held[...] -= dot3(product3[slot, 0], solved[k - 1, 0]).reshape(2, hb, width)
             take_solved(k - 1, 1)
 
         for h in range(2):
@@ -345,10 +341,6 @@
 
     lax.fori_loop(0, rows * chunks * 2, take, 0)
 
-    @pl.when(z > 0)
-    def _():
-        subtract(0)
-
     def step(k, carry):
         root = lax.rem(k, rows)
         is_root = z == root
@@ -356,9 +348,21 @@
 
         @pl.when(is_root)
         def _():
+            @pl.when((k > 0) & (k < rows))
+            def _():
+                subtract(0)
+
             @pl.when(k > 0)
             def _():
                 solve(k, k // rows)
+
+            @pl.when(k < rows)
+            def _():
+                def later(j, carry):
+                    update(j, 1)
+                    return carry
+
+                lax.fori_loop(0, k + 1, later, 0)
 
         @pl.when(jnp.logical_and(needs(k, z), jnp.logical_not(is_root | is_next)))
         def _():
@@ -369,11 +373,7 @@
         def _():
             update(k, 0)
 
-        @pl.when(jnp.logical_and(is_root, (k > 0) & (k < rows)))
-        def _():
-            update(k - 1, 1)
-
-        @pl.when(jnp.logical_or(jnp.logical_not(is_root | is_next), is_root & (k < rows)))
+        @pl.when(jnp.logical_not(is_root | is_next) & (z < k))
         def _():
             update(k, 1)
 

time: 74.6 us -> 74.5 us (level)
  no operation moved by 1% of the time
where the time goes in v6:
time: 74.5 us; the launch traced here: 74 us
  Pallas kernels  72.3 us (97%)
  local copies, waits for them, and re-layouts  1.67 us (2%)
    pallas_call x1, Pallas kernels, kernel_body(): pl.pallas_call(functools.partial(kernel, rows, cols, slots, bk, chunks, w...  72.3 us
    unnamed x1, local copies, waits for them, and re-layouts  1.67 us

profile of v6, /device:TPU:27, one launch (start us, length us, event | category | flops | bytes accessed | tf_op | source)
XLA Modules:
  0.0 74.0 jit_solution(6243570950640589222)
XLA Ops:
  0.0 72.3 %shard_map.46 = f32[512,128]{1,0:T(8,128)} custom-call(f32[512,512]{1,0:T(8,128)} %right_ref.1, f32[512,1024]{1,0:T(8,128)} %factor_ref.1, f32[1024,128]{1,0:T(8,128)} %solution_ref.1, f32[512,1536]{1,0:T(8,128)} %window_ref.1), custom_call_target="tpu_custom_call" | custom-call | tf_op jit(solution)/shard_map/pallas_call | solution.py:440
  72.3 1.7 %copy.6 = f32[512,128]{1,0:T(8,128)} copy(f32[512,128]{1,0:T(8,128)} %shard_map.46) | data formatting | bytes 524288

commit v7 on v6

--- a/solution.py
+++ b/solution.py
@@ -253,6 +253,13 @@
         def _():
             send_solved(k, h, z + 1).start()
 
+        @pl.when(passes_left(k, root))
+        def _():
+            send_solved(k, h, z - 1).start()
+
+    def passes_left(k, root):
+        return (z < root) & (z > 0) & (root < rows - 1) & needs(k, z - 1)
+
     def solve(k, slot):
         root = lax.rem(k, rows)
         held[...] = dot3(window3[k, slot], resid[slot]).reshape(2, hb, width)
@@ -287,7 +294,8 @@
                     send_solved(k, h, dest).start()
 
     def others(k, root, dest):
-        side = (dest < root) | ((dest > root) & (k == STEPS - 1))
+        left = (dest < root) & ((dest == root - 1) | (root == rows - 1))
+        side = left | ((dest > root) & (k == STEPS - 1))
         return side & (first_dest(k, root) != dest) & needs(k, dest)
 
     def update(k, slot):
@@ -418,6 +426,7 @@
         middle = (z > root) & (z < rows - 1) & (k < STEPS - 1)
         for dest in range(rows):
             near = (start & (first_dest(k, root) == dest)) | (middle & (dest == z + 1))
+            near = near | (passes_left(k, root) & (dest == z - 1))
 
             @pl.when((near | ((z == root) & others(k, root, dest))) & (z != dest))
             def _():

time: 74.5 us -> 74.6 us (level)
  no operation moved by 1% of the time
where the time goes in v7:
time: 74.6 us; the launch traced here: 74.2 us
  Pallas kernels  72.5 us (97%)
  local copies, waits for them, and re-layouts  1.67 us (2%)
    pallas_call x1, Pallas kernels, kernel_body(): pl.pallas_call(functools.partial(kernel, rows, cols, slots, bk, chunks, w...  72.5 us
    unnamed x1, local copies, waits for them, and re-layouts  1.67 us

profile of v7, /device:TPU:27, one launch (start us, length us, event | category | flops | bytes accessed | tf_op | source)
XLA Modules:
  0.0 74.2 jit_solution(8707854757307069432)
XLA Ops:
  0.0 72.5 %shard_map.46 = f32[512,128]{1,0:T(8,128)} custom-call(f32[512,512]{1,0:T(8,128)} %right_ref.1, f32[512,1024]{1,0:T(8,128)} %factor_ref.1, f32[1024,128]{1,0:T(8,128)} %solution_ref.1, f32[512,1536]{1,0:T(8,128)} %window_ref.1), custom_call_target="tpu_custom_call" | custom-call | tf_op jit(solution)/shard_map/pallas_call | solution.py:449
  72.5 1.7 %copy.6 = f32[512,128]{1,0:T(8,128)} copy(f32[512,128]{1,0:T(8,128)} %shard_map.46) | data formatting | bytes 524288

commit v8 on v6

--- a/solution.py
+++ b/solution.py
@@ -328,11 +328,11 @@
         before = s + (1 - 2 * way)
         twice = (distance == 1) & (way == 1)
 
-        @pl.when((q == 1) & (before >= 0) & (before < rows) & jnp.logical_not(twice))
+        @pl.when((q == chunks // 4) & (before >= 0) & (before < rows) & jnp.logical_not(twice))
         def _():
             push_later(before)
 
-        @pl.when((z == 0) & (c == distance - 1) & (q == 2) & (way == 0))
+        @pl.when((z == 0) & (c == distance - 1) & (q == chunks // 2) & (way == 0))
         def _():
             subtract(0)
             solve(0, 0)
@@ -433,7 +433,7 @@
     bk = window_factor.shape[1] // STEPS
     slots = right_side.shape[0] // bk
     width = right_side.shape[1] // cols
-    chunks = 4
+    chunks = 8
     depth = prev_factor.shape[1] // chunks
     height = slots * bk
     f32, bf16 = jnp.float32, jnp.bfloat16
@@ -482,7 +482,7 @@
             and rows < STEPS < 2 * rows
             and width % 128 == 0
             and bk % 256 == 0
-            and prev_factor.shape[1] % 512 == 0
+            and prev_factor.shape[1] % 1024 == 0
         )
         if fits:
             return kernel_body(rows, cols, right_side, prev_factor, prev_solution, window_factor)

time: 74.5 us -> 75.4 us (1.012)
  Pallas kernels: 72.3 us -> 73.2 us
    pallas_call x1, Pallas kernels: 72.3 us -> 73.2 us  [kernel_body(): pl.pallas_call(functools.partial(kernel, rows, cols, slots, bk, chunks, w...]
where the time goes in v8:
time: 75.4 us; the launch traced here: 74.9 us
  Pallas kernels  73.2 us (97%)
  local copies, waits for them, and re-layouts  1.67 us (2%)
    pallas_call x1, Pallas kernels, kernel_body(): pl.pallas_call(functools.partial(kernel, rows, cols, slots, bk, chunks, w...  73.2 us
    unnamed x1, local copies, waits for them, and re-layouts  1.67 us

profile of v8, /device:TPU:27, one launch (start us, length us, event | category | flops | bytes accessed | tf_op | source)
XLA Modules:
  0.0 74.9 jit_solution(14009499011394886856)
XLA Ops:
  0.0 73.2 %shard_map.46 = f32[512,128]{1,0:T(8,128)} custom-call(f32[512,512]{1,0:T(8,128)} %right_ref.1, f32[512,1024]{1,0:T(8,128)} %factor_ref.1, f32[1024,128]{1,0:T(8,128)} %solution_ref.1, f32[512,1536]{1,0:T(8,128)} %window_ref.1), custom_call_target="tpu_custom_call" | custom-call | tf_op jit(solution)/shard_map/pallas_call | solution.py:440
  73.2 1.7 %copy.6 = f32[512,128]{1,0:T(8,128)} copy(f32[512,128]{1,0:T(8,128)} %shard_map.46) | data formatting | bytes 524288

commit v9 on v6

--- a/solution.py
+++ b/solution.py
@@ -332,7 +332,7 @@
         def _():
             push_later(before)
 
-        @pl.when((z == 0) & (c == distance - 1) & (q == 2) & (way == 0))
+        @pl.when((z == 0) & (c == distance - 1) & (q == chunks // 2) & (way == 0))
         def _():
             subtract(0)
             solve(0, 0)
@@ -433,7 +433,7 @@
     bk = window_factor.shape[1] // STEPS
     slots = right_side.shape[0] // bk
     width = right_side.shape[1] // cols
-    chunks = 4
+    chunks = 2
     depth = prev_factor.shape[1] // chunks
     height = slots * bk
     f32, bf16 = jnp.float32, jnp.bfloat16

time: 74.5 us -> 74.2 us (level)
  no operation moved by 1% of the time
where the time goes in v9:
time: 74.2 us; the launch traced here: 73.7 us
  Pallas kernels  72 us (97%)
  local copies, waits for them, and re-layouts  1.67 us (2%)
    pallas_call x1, Pallas kernels, kernel_body(): pl.pallas_call(functools.partial(kernel, rows, cols, slots, bk, chunks, w...  72 us
    unnamed x1, local copies, waits for them, and re-layouts  1.67 us

profile of v9, /device:TPU:27, one launch (start us, length us, event | category | flops | bytes accessed | tf_op | source)
XLA Modules:
  0.0 73.7 jit_solution(11746262233384833391)
XLA Ops:
  0.0 72.0 %shard_map.46 = f32[512,128]{1,0:T(8,128)} custom-call(f32[512,512]{1,0:T(8,128)} %right_ref.1, f32[512,1024]{1,0:T(8,128)} %factor_ref.1, f32[1024,128]{1,0:T(8,128)} %solution_ref.1, f32[512,1536]{1,0:T(8,128)} %window_ref.1), custom_call_target="tpu_custom_call" | custom-call | tf_op jit(solution)/shard_map/pallas_call | solution.py:440
  72.0 1.7 %copy.6 = f32[512,128]{1,0:T(8,128)} copy(f32[512,128]{1,0:T(8,128)} %shard_map.46) | data formatting | bytes 524288
